TPU v7x, 32 devices: a whole 2x2x4 slice. The times are simulated.
32 devices in a mesh: grp: 8 (over z, x), rep: 4 (over y, core).
Axes of the slice: x: 2, y: 2, z: 4, core: 2. Of those that a mesh axis runs over, the one named last changes fastest.
Arguments:
- series: bfloat16 [256, 5632], P('grp'), may hold values from -6 to 6
- regressors: float32 [256, 24], P('grp'), may hold values from -3 to 3
- span_ids: int32 [256], replicated, may hold values from 0 to 3, never falling along the last dimension, each value on 1 to 128 neighbouring positions
- nuisance_count: int32 [1], replicated, may hold values from 12 to 24
- owner_order: int32 [8], replicated, may hold values from 0 to 7
- vectors: bfloat16 [5632, 64], P('grp'), may hold values from -0.3125 to 0.3125
Outputs:
- projected: float32 [5632, 64], P(('grp', 'rep'))
Inputs may be any that keep to these rules, and one draw needn't show every extreme that they name: `span_ids`: never falls along frames; each of the 4 spans holds 1 to 128 frames, one exactly 128. `owner_order`: blocks may name the same slab.
All inputs are finite; a program needn't handle non-finite values.
Results may differ from a plain program's by a relative error of at most 0.0095.
Values may be sent and summed in bfloat16 or wider, within the bound.
A program may use at most 64 MiB of HBM per device.

v0:
```python
import math
import jax
import jax.numpy as jnp
from jax import lax
from jax.sharding import PartitionSpec as P

BLOCKS = 8
fast_pole = 0.64
slow_pole = 0.955
corr_limit = 0.99
norm_eps = 1e-06


def spread_2(value, axis, root):
    mine = lax.axis_index(axis) == root
    return lax.psum(jnp.where(mine, value, jnp.zeros_like(value)), axis)


def fisher_map(correlation):
    clipped = jnp.clip(correlation, -corr_limit, corr_limit)
    return 0.5 * jnp.log((1.0 + clipped) / (1.0 - clipped))


def block_operators(span_ids, frames):
    offsets = jnp.arange(128)
    lag_steps = offsets[:, None] - offsets[None, :]
    lag_clip = jnp.maximum(lag_steps, 0).astype(jnp.float32)
    operators = []
    for number in range(frames // 128):
        ids_here = span_ids[number * 128 : (number + 1) * 128]
        joined = (ids_here[:, None] == ids_here[None, :]) & (lag_steps >= 0)
        if number == 0:
            linked = jnp.zeros((128,), jnp.float32)
        else:
            linked = (ids_here == span_ids[number * 128 - 1]).astype(jnp.float32)
        pole_pair = []
        for pole_value in (fast_pole, slow_pole):
            matrix = jnp.where(
                joined, (1.0 - pole_value) * jnp.exp(lag_clip * math.log(pole_value)), 0.0
            )
            carried = linked * jnp.exp((offsets + 1).astype(jnp.float32) * math.log(pole_value))
            pole_pair.append((matrix, carried))
        operators.append(pole_pair)
    return operators


def band_pass(columns_in, operators):
    col_count = columns_in.shape[1]
    states = [jnp.zeros((col_count,), jnp.float32), jnp.zeros((col_count,), jnp.float32)]
    pieces = []
    for number, pole_pair in enumerate(operators):
        segment = columns_in[number * 128 : (number + 1) * 128]
        outputs = []
        for pole_slot in range(2):
            matrix, carried = pole_pair[pole_slot]
            response = (
                jnp.dot(matrix, segment, precision=lax.Precision.HIGHEST)
                + carried[:, None] * states[pole_slot][None, :]
            )
            states[pole_slot] = response[-1]
            outputs.append(response)
        pieces.append(outputs[0] - outputs[1])
    return jnp.concatenate(pieces, axis=0)


def nuisance_basis(filtered_nuisance, nuisance_count):
    active = (jnp.arange(filtered_nuisance.shape[1]) < nuisance_count[0]).astype(jnp.float32)
    masked = filtered_nuisance * active[None, :]
    gram_matrix = jnp.dot(masked.T, masked, precision=lax.Precision.HIGHEST) + jnp.diag(
        1.0 - active
    )
    return (masked, jnp.linalg.cholesky(gram_matrix))


def scale_columns(filtered, masked, lower_factor):
    highest = lax.Precision.HIGHEST
    right_side = jnp.dot(masked.T, filtered, precision=highest)
    halfway = lax.linalg.triangular_solve(lower_factor, right_side, left_side=True, lower=True)
    coefficients = lax.linalg.triangular_solve(
        lower_factor, halfway, left_side=True, lower=True, transpose_a=True
    )
    cleaned = filtered - jnp.dot(masked, coefficients, precision=highest)
    centered = cleaned - jnp.mean(cleaned, axis=0, keepdims=True)
    spread = lax.rsqrt(jnp.mean(centered * centered, axis=0, keepdims=True) + norm_eps)
    return (centered * spread * (1.0 / math.sqrt(centered.shape[0]))).astype(jnp.bfloat16)


def fold_tile(my_cols, vec_slab, running, part_cols):
    correlation = lax.dot_general(
        my_cols, part_cols, (((0,), (0,)), ((), ())), preferred_element_type=jnp.float32
    )
    fisher = fisher_map(correlation).astype(jnp.bfloat16)
    return running + jnp.dot(fisher, vec_slab, preferred_element_type=jnp.float32)


def local(series, regressors, span_ids, nuisance_count, owner_order, vectors):
    grp_count = lax.axis_size("grp")
    rep_count = lax.axis_size("rep")
    rep_index = lax.axis_index("rep")
    frames_loc = series.shape[0]
    frames = frames_loc * grp_count
    own_cols = series.shape[1] // (grp_count * rep_count)
    operators = block_operators(span_ids, frames)
    nuisance = lax.all_gather(regressors, "grp", axis=0, tiled=True)
    masked, lower_factor = nuisance_basis(band_pass(nuisance, operators), nuisance_count)
    quarter = series.reshape(frames_loc, grp_count, rep_count, own_cols)
    quarter = lax.dynamic_slice_in_dim(quarter, rep_index, 1, 2).reshape(
        frames_loc, grp_count, own_cols
    )
    filtered = band_pass(
        lax.all_to_all(quarter, "grp", split_axis=1, concat_axis=0, tiled=True)[:, 0, :].astype(
            jnp.float32
        ),
        operators,
    )
    unit_cols = scale_columns(filtered, masked, lower_factor)
    projected = jnp.zeros((own_cols, vectors.shape[1]), jnp.float32)
    for number in range(BLOCKS):
        piece_in, vec_slab = (
            spread_2(unit_cols, "grp", owner_order[number]),
            spread_2(vectors, "grp", owner_order[number]),
        )
        projected = fold_tile(
            unit_cols, vec_slab, projected, lax.all_gather(piece_in, "rep", axis=1, tiled=True)
        )
    return projected


def solution(mesh):
    placed = (P("grp", None), P("grp", None), P(), P(), P(), P("grp", None))
    return jax.shard_map(
        local, mesh=mesh, in_specs=placed, out_specs=P(("grp", "rep"), None), check_vma=False
    )
```

profile of v0, /device:TPU:0, one launch (start us, length us, event | category | flops | bytes accessed | tf_op | source)
XLA Modules:
  0.0 231.1 jit_solution(4362847719951692597)
XLA Ops:
  6.5 2.0 reshape.62
  8.8 0.7 copy.24
  9.6 7.3 %all-to-all-start = ((bf16[32,8,176]{2,0,1:T(8,128)(2,1)}), bf16[32,8,176]{2,0,1:T(8,128)(2,1)S(1)}, u32[]{:S(2)}, u32[]{:S(2)}) async-start(bf16[32,8,176]{2,0,1:T(8,128)(2,1)} %bitcast.70), calls=%async_computation | async-start | bytes 262144 | tf_op jit(solution)/shard_map/all_to_all | solution.py:111
  16.9 0.7 copy-done.10
  17.5 0.6 slice.91
  18.8 0.7 compare_select_fusion
  19.5 0.7 fusion.173
  25.2 31.1 %all-gather = f32[8,32,24]{1,2,0:T(8,128)S(1)} all-gather(f32[1,32,24]{1,2,0:T(8,128)S(1)} %bitcast.78), channel_id=1, replica_groups=mesh['grp'=8,'rep'=4] {'grp'}, dimensions={0}, use_global_device_ids=true | all-gather | bytes 27648 | tf_op jit(solution)/shard_map/all_gather | solution.py:104
  58.4 2.2 cholesky.16
  60.7 0.6 compare_reduce_fusion
  61.3 0.6 fusion.93
  62.0 1.9 custom-call.8
  63.8 0.9 broadcast_select_fusion
  67.6 0.8 broadcast_select_fusion.8
  68.4 0.9 broadcast_select_fusion.9
  69.3 95.1 %all-reduce.3.cloned.1.call-done = (bf16[704,64]{0,1:T(8,128)(2,1)}, bf16[256,176]{0,1:T(8,128)(2,1)}, bf16[704,64]{0,1:T(8,128)(2,1)}, bf16[256,176]{0,1:T(8,12...) async-done(((bf16[704,64]{0,1:T(8,128)(2,1)}, ...) | async-done | bytes 1441808 | tf_op jit(solution)/shard_map/psum | solution.py:16
  164.5 6.7 %all_gather.28 = bf16[256,704]{0,1:T(8,128)(2,1)S(1)} all-gather(bf16[256,176]{0,1:T(8,128)(2,1)} %get-tuple-element.6), channel_id=1, replica_groups=mesh['grp'=8,'rep'=4] {'rep'}, dimensions={1}, use_global_device_ids=true | all-gather | bytes 450560 | tf_op jit(solution)/shard_map/all_gather | solution.py:124
  171.2 6.5 %all_gather.29 = bf16[256,704]{0,1:T(8,128)(2,1)S(1)} all-gather(bf16[256,176]{0,1:T(8,128)(2,1)S(1)} %copy-done.7), channel_id=1, replica_groups=mesh['grp'=8,'rep'=4] {'rep'}, dimensions={1}, use_global_device_ids=true | all-gather | bytes 450560 | tf_op jit(solution)/shard_map/all_gather | solution.py:124
  177.7 6.5 %all_gather.30 = bf16[256,704]{0,1:T(8,128)(2,1)S(1)} all-gather(bf16[256,176]{0,1:T(8,128)(2,1)S(1)} %copy-done.6), channel_id=1, replica_groups=mesh['grp'=8,'rep'=4] {'rep'}, dimensions={1}, use_global_device_ids=true | all-gather | bytes 450560 | tf_op jit(solution)/shard_map/all_gather | solution.py:124
  184.2 6.5 %all_gather.31 = bf16[256,704]{0,1:T(8,128)(2,1)S(1)} all-gather(bf16[256,176]{0,1:T(8,128)(2,1)S(1)} %copy-done.5), channel_id=1, replica_groups=mesh['grp'=8,'rep'=4] {'rep'}, dimensions={1}, use_global_device_ids=true | all-gather | bytes 450560 | tf_op jit(solution)/shard_map/all_gather | solution.py:124
  190.7 6.5 %all_gather.32 = bf16[256,704]{0,1:T(8,128)(2,1)S(1)} all-gather(bf16[256,176]{0,1:T(8,128)(2,1)S(1)} %copy-done.4), channel_id=1, replica_groups=mesh['grp'=8,'rep'=4] {'rep'}, dimensions={1}, use_global_device_ids=true | all-gather | bytes 450560 | tf_op jit(solution)/shard_map/all_gather | solution.py:124
  197.3 6.5 %all_gather.33 = bf16[256,704]{0,1:T(8,128)(2,1)S(1)} all-gather(bf16[256,176]{0,1:T(8,128)(2,1)S(1)} %copy-done.3), channel_id=1, replica_groups=mesh['grp'=8,'rep'=4] {'rep'}, dimensions={1}, use_global_device_ids=true | all-gather | bytes 450560 | tf_op jit(solution)/shard_map/all_gather | solution.py:124
  203.8 6.5 %all_gather.34 = bf16[256,704]{0,1:T(8,128)(2,1)S(1)} all-gather(bf16[256,176]{0,1:T(8,128)(2,1)S(1)} %copy-done.2), channel_id=1, replica_groups=mesh['grp'=8,'rep'=4] {'rep'}, dimensions={1}, use_global_device_ids=true | all-gather | bytes 450560 | tf_op jit(solution)/shard_map/all_gather | solution.py:124
  210.3 6.5 %all_gather.35 = bf16[256,704]{0,1:T(8,128)(2,1)S(1)} all-gather(bf16[256,176]{0,1:T(8,128)(2,1)S(1)} %copy-done.1), channel_id=1, replica_groups=mesh['grp'=8,'rep'=4] {'rep'}, dimensions={1}, use_global_device_ids=true | all-gather | bytes 450560 | tf_op jit(solution)/shard_map/all_gather | solution.py:124
  216.8 0.5 fusion.2
  217.7 0.5 convolution_add_fusion.10
  218.6 0.5 convolution_add_fusion.9
  219.5 0.5 convolution_add_fusion.8
  220.4 0.5 convolution_add_fusion.7
  221.3 0.5 convolution_add_fusion.6
  222.2 0.5 convolution_add_fusion.5
  223.1 1.1 convolution_add_fusion.4
  (75 shorter events, 8.0 us)
Async XLA Ops:
  9.6 55.2 %all-to-all-start = ((bf16[32,8,176]{2,0,1:T(8,128)(2,1)}), bf16[32,8,176]{2,0,1:T(8,128)(2,1)S(1)}, u32[]{:S(2)}, u32[]{:S(2)}) async-start(bf16[32,8,176]{2,0,1:T(8,128)(2,1)} %bitcast.70), calls=%async_computation | async-start | bytes 262144 | tf_op jit(solution)/shard_map/all_to_all | solution.py:111
  16.8 147.6 %all-reduce.3.cloned.1.call-start = ((), (), s32[]{:S(2)}) async-start(), calls=%async_computation.1 | async-start | bytes 3014656 | tf_op jit(solution)/shard_map/psum | solution.py:16
  16.9 0.7 copy-start.10
  18.8 0.7 copy-start.8
  22.6 2.6 %copy-start.9 = (f32[32,24]{0,1:T(8,128)S(1)}, f32[32,24]{0,1:T(8,128)}, u32[]{:S(2)}) copy-start(f32[32,24]{0,1:T(8,128)} %param.7) | copy-start | bytes 9220
  58.1 5.8 %copy-start = (bf16[704,64]{0,1:T(8,128)(2,1)S(1)}, bf16[704,64]{0,1:T(8,128)(2,1)}, u32[]{:S(2)}) copy-start(bf16[704,64]{0,1:T(8,128)(2,1)} %param.11) | copy-start | bytes 270340
  164.5 6.7 %copy-start.7 = (bf16[256,176]{0,1:T(8,128)(2,1)S(1)}, bf16[256,176]{0,1:T(8,128)(2,1)}, u32[]{:S(2)}) copy-start(bf16[256,176]{0,1:T(8,128)(2,1)} %get-tuple-element.8) | copy-start | bytes 270340
  171.2 6.5 %copy-start.6 = (bf16[256,176]{0,1:T(8,128)(2,1)S(1)}, bf16[256,176]{0,1:T(8,128)(2,1)}, u32[]{:S(2)}) copy-start(bf16[256,176]{0,1:T(8,128)(2,1)} %get-tuple-element.10) | copy-start | bytes 270340
  177.7 6.5 %copy-start.5 = (bf16[256,176]{0,1:T(8,128)(2,1)S(1)}, bf16[256,176]{0,1:T(8,128)(2,1)}, u32[]{:S(2)}) copy-start(bf16[256,176]{0,1:T(8,128)(2,1)} %get-tuple-element.12) | copy-start | bytes 270340
  184.2 6.5 %copy-start.4 = (bf16[256,176]{0,1:T(8,128)(2,1)S(1)}, bf16[256,176]{0,1:T(8,128)(2,1)}, u32[]{:S(2)}) copy-start(bf16[256,176]{0,1:T(8,128)(2,1)} %get-tuple-element.14) | copy-start | bytes 270340
  190.7 6.5 %copy-start.3 = (bf16[256,176]{0,1:T(8,128)(2,1)S(1)}, bf16[256,176]{0,1:T(8,128)(2,1)}, u32[]{:S(2)}) copy-start(bf16[256,176]{0,1:T(8,128)(2,1)} %get-tuple-element.16) | copy-start | bytes 270340
  197.3 6.5 %copy-start.2 = (bf16[256,176]{0,1:T(8,128)(2,1)S(1)}, bf16[256,176]{0,1:T(8,128)(2,1)}, u32[]{:S(2)}) copy-start(bf16[256,176]{0,1:T(8,128)(2,1)} %get-tuple-element.18) | copy-start | bytes 270340
  203.8 6.5 %copy-start.1 = (bf16[256,176]{0,1:T(8,128)(2,1)S(1)}, bf16[256,176]{0,1:T(8,128)(2,1)}, u32[]{:S(2)}) copy-start(bf16[256,176]{0,1:T(8,128)(2,1)} %get-tuple-element.20) | copy-start | bytes 270340
  210.3 6.5 %copy-start.18 = (bf16[704,64]{0,1:T(8,128)(2,1)S(1)}, bf16[704,64]{0,1:T(8,128)(2,1)}, u32[]{:S(2)}) copy-start(bf16[704,64]{0,1:T(8,128)(2,1)} %get-tuple-element.5) | copy-start | bytes 270340
  216.8 0.9 copy-start.17
  217.7 0.9 copy-start.16
  218.6 0.9 copy-start.15
  219.5 0.9 copy-start.14
  220.4 0.9 copy-start.13
  221.3 0.9 copy-start.12
  222.2 0.9 copy-start.11
Sparse Core Ops, SparseCore 0:
  69.4 94.9 all-reduce.2
where the time goes:
time: 232 us; the launch traced here: 231 us
  waiting for transfers between devices  95.1 us (41%)
  blocking collectives  83.4 us (36%)
  between operations  19.4 us (8%)
  other arithmetic  8.9 us (4%)
  local copies, waits for them, and re-layouts  8.67 us (4%)
  matrix products  8.23 us (4%)
  starting transfers between devices  7.29 us (3%)
    psum x1, waiting for transfers between devices, spread_2(): return lax.psum(jnp.where(mine, value, jnp.zeros_like(value)), axis)  95.1 us
    all_gather x8, blocking collectives, local(): lax.all_gather(piece_in, 'rep', axis=1, tiled=True)  52.3 us
    all_gather x1, blocking collectives, local(): nuisance = lax.all_gather(regressors, 'grp', axis=0, tiled=True)  31.1 us
    all_to_all x1, starting transfers between devices, local(): lax.all_to_all(quarter, 'grp', split_axis=1, concat_axis=0, tiled=True)  7.25 us
    dot_general x8, matrix products, fold_tile(): jnp.dot(fisher, vec_slab, preferred_element_type=jnp.float32)  4.66 us
  transfers between devices with their start and end apart: 2, of which 1 were waited for; matrix products, arithmetic and copies ran while one was open for 4% of the time, Pallas kernels for 0%

commit v1 on v0

--- a/solution.py
+++ b/solution.py
@@ -13,7 +13,7 @@
 
 def spread_2(value, axis, root):
     mine = lax.axis_index(axis) == root
-    return lax.psum(jnp.where(mine, value, jnp.zeros_like(value)), axis)
+    return jnp.sum(lax.all_gather(jnp.where(mine, value, jnp.zeros_like(value)), axis), axis=0)
 
 
 def fisher_map(correlation):

time: 232 us -> 649 us (2.80)
  blocking collectives: 83.4 us -> 601 us
  waiting for transfers between devices: 95.1 us -> 0.01 us
  between operations: 19.4 us -> 6.12 us
    all_gather x0 -> x16, blocking collectives: none -> 521 us  [spread_2(): lax.all_gather(jnp.where(mine, value, jnp.zeros_like(value)), axis)]
    psum x1 -> x0, waiting for transfers between devices: 95.1 us -> none  [spread_2(): return lax.psum(jnp.where(mine, value, jnp.zeros_like(value)), axis)]
    reduce_sum x0 -> x16, other arithmetic: none -> 8.4 us  [spread_2(): jnp.sum(lax.all_gather(jnp.where(mine, value, jnp.zeros_like(value)), axi...]
  transfers between devices with their start and end apart: 2 -> 1, of which waited for: 1 -> 0; matrix products, arithmetic and copies ran while one was open for 4% -> 2% of each run, Pallas kernels for 0% -> 0%
where the time goes in v1:
time: 649 us; the launch traced here: 648 us
  blocking collectives  601 us (93%)
  other arithmetic  14.9 us (2%)
  local copies, waits for them, and re-layouts  10.5 us (2%)
  matrix products  8.22 us (1%)
  starting transfers between devices  7.38 us (1%)
    all_gather x16, blocking collectives, spread_2(): lax.all_gather(jnp.where(mine, value, jnp.zeros_like(value)), axis)  521 us
    all_gather x8, blocking collectives, local(): lax.all_gather(piece_in, 'rep', axis=1, tiled=True)  48.6 us
    all_gather x1, blocking collectives, local(): nuisance = lax.all_gather(regressors, 'grp', axis=0, tiled=True)  31.1 us
  transfers between devices with their start and end apart: 1, of which 0 were waited for; matrix products, arithmetic and copies ran while one was open for 2% of the time, Pallas kernels for 0%

profile of v1, /device:TPU:0, one launch (start us, length us, event | category | flops | bytes accessed | tf_op | source)
XLA Modules:
  0.0 647.8 jit_solution(716471465655234668)
XLA Ops:
  0.0 2.0 reshape.62
  3.0 7.4 %all-to-all-start = ((bf16[32,8,176]{2,0,1:T(8,128)(2,1)}), bf16[32,8,176]{2,0,1:T(8,128)(2,1)S(1)}, u32[]{:S(2)}, u32[]{:S(2)}) async-start(bf16[32,8,176]{2,0,1:T(8,128)(2,1)} %bitcast.126), calls=%async_computation | async-start | bytes 262144 | tf_op jit(solution)/shard_map/all_to_all | solution.py:111
  11.7 31.1 %all-gather.16 = f32[8,32,24]{1,2,0:T(8,128)S(1)} all-gather(f32[1,32,24]{1,2,0:T(8,128)S(1)} %bitcast.142), channel_id=1, replica_groups=mesh['grp'=8,'rep'=4] {'grp'}, dimensions={0}, use_global_device_ids=true | all-gather | bytes 27648 | tf_op jit(solution)/shard_map/all_gather | solution.py:104
  46.3 2.2 cholesky.16
  55.5 32.1 %all-gather.17 = bf16[8,704,64]{1,2,0:T(8,128)(2,1)S(1)} all-gather(bf16[1,704,64]{1,2,0:T(8,128)(2,1)S(1)} %get-tuple-element.15), channel_id=3, replica_groups=mesh['grp'=8,'rep'=4] {'grp'}, dimensions={0}, use_global_device_ids=true | all-gather | bytes 811008 | tf_op jit(solution)/shard_map/all_gather | solution.py:16
  87.6 32.6 %all-gather.18 = bf16[8,704,64]{1,2,0:T(8,128)(2,1)S(1)} all-gather(bf16[1,704,64]{1,2,0:T(8,128)(2,1)S(1)} %get-tuple-element.14), channel_id=5, replica_groups=mesh['grp'=8,'rep'=4] {'grp'}, dimensions={0}, use_global_device_ids=true | all-gather | bytes 811008 | tf_op jit(solution)/shard_map/all_gather | solution.py:16
  120.2 32.4 %all-gather.19 = bf16[8,704,64]{1,2,0:T(8,128)(2,1)S(1)} all-gather(bf16[1,704,64]{1,2,0:T(8,128)(2,1)S(1)} %get-tuple-element.13), channel_id=7, replica_groups=mesh['grp'=8,'rep'=4] {'grp'}, dimensions={0}, use_global_device_ids=true | all-gather | bytes 811008 | tf_op jit(solution)/shard_map/all_gather | solution.py:16
  152.6 31.7 %all-gather.20 = bf16[8,704,64]{1,2,0:T(8,128)(2,1)S(1)} all-gather(bf16[1,704,64]{1,2,0:T(8,128)(2,1)S(1)} %get-tuple-element.12), channel_id=9, replica_groups=mesh['grp'=8,'rep'=4] {'grp'}, dimensions={0}, use_global_device_ids=true | all-gather | bytes 811008 | tf_op jit(solution)/shard_map/all_gather | solution.py:16
  184.3 34.4 %all-gather.21 = bf16[8,704,64]{1,2,0:T(8,128)(2,1)} all-gather(bf16[1,704,64]{1,2,0:T(8,128)(2,1)S(1)} %get-tuple-element.11), channel_id=11, replica_groups=mesh['grp'=8,'rep'=4] {'grp'}, dimensions={0}, use_global_device_ids=true | all-gather | bytes 811008 | tf_op jit(solution)/shard_map/all_gather | solution.py:16
  218.7 34.3 %all-gather.22 = bf16[8,704,64]{1,2,0:T(8,128)(2,1)} all-gather(bf16[1,704,64]{1,2,0:T(8,128)(2,1)S(1)} %get-tuple-element.10), channel_id=13, replica_groups=mesh['grp'=8,'rep'=4] {'grp'}, dimensions={0}, use_global_device_ids=true | all-gather | bytes 811008 | tf_op jit(solution)/shard_map/all_gather | solution.py:16
  253.1 34.1 %all-gather.23 = bf16[8,704,64]{1,2,0:T(8,128)(2,1)} all-gather(bf16[1,704,64]{1,2,0:T(8,128)(2,1)S(1)} %get-tuple-element.16), channel_id=15, replica_groups=mesh['grp'=8,'rep'=4] {'grp'}, dimensions={0}, use_global_device_ids=true | all-gather | bytes 811008 | tf_op jit(solution)/shard_map/all_gather | solution.py:16
  287.2 34.4 %all-gather.24 = bf16[8,704,64]{1,2,0:T(8,128)(2,1)} all-gather(bf16[1,704,64]{1,2,0:T(8,128)(2,1)S(1)} %get-tuple-element.9), channel_id=17, replica_groups=mesh['grp'=8,'rep'=4] {'grp'}, dimensions={0}, use_global_device_ids=true | all-gather | bytes 811008 | tf_op jit(solution)/shard_map/all_gather | solution.py:16
  322.2 1.8 custom-call.8
  324.0 0.8 reduce_sum.213
  327.0 0.8 reduce_sum.221
  332.2 31.5 %all-gather = bf16[2048,176]{0,1:T(8,128)(2,1)S(1)} all-gather(bf16[256,176]{0,1:T(8,128)(2,1)S(1)} %get-tuple-element.25), channel_id=2, replica_groups=mesh['grp'=8,'rep'=4] {'grp'}, dimensions={0}, use_global_device_ids=true | all-gather | bytes 811008 | tf_op jit(solution)/shard_map/all_gather | solution.py:16
  364.5 6.1 all_gather.126
  370.5 31.7 %all-gather.2 = bf16[2048,176]{0,1:T(8,128)(2,1)S(1)} all-gather(bf16[256,176]{0,1:T(8,128)(2,1)S(1)} %get-tuple-element.24), channel_id=4, replica_groups=mesh['grp'=8,'rep'=4] {'grp'}, dimensions={0}, use_global_device_ids=true | all-gather | bytes 811008 | tf_op jit(solution)/shard_map/all_gather | solution.py:16
  402.9 6.1 all_gather.131
  409.0 31.9 %all-gather.4 = bf16[2048,176]{0,1:T(8,128)(2,1)S(1)} all-gather(bf16[256,176]{0,1:T(8,128)(2,1)S(1)} %get-tuple-element.23), channel_id=6, replica_groups=mesh['grp'=8,'rep'=4] {'grp'}, dimensions={0}, use_global_device_ids=true | all-gather | bytes 811008 | tf_op jit(solution)/shard_map/all_gather | solution.py:16
  441.6 6.1 all_gather.136
  447.7 32.1 %all-gather.6 = bf16[2048,176]{0,1:T(8,128)(2,1)S(1)} all-gather(bf16[256,176]{0,1:T(8,128)(2,1)S(1)} %get-tuple-element.22), channel_id=8, replica_groups=mesh['grp'=8,'rep'=4] {'grp'}, dimensions={0}, use_global_device_ids=true | all-gather | bytes 811008 | tf_op jit(solution)/shard_map/all_gather | solution.py:16
  480.5 6.1 all_gather.141
  486.6 31.9 %all-gather.8 = bf16[2048,176]{0,1:T(8,128)(2,1)S(1)} all-gather(bf16[256,176]{0,1:T(8,128)(2,1)S(1)} %get-tuple-element.21), channel_id=10, replica_groups=mesh['grp'=8,'rep'=4] {'grp'}, dimensions={0}, use_global_device_ids=true | all-gather | bytes 811008 | tf_op jit(solution)/shard_map/all_gather | solution.py:16
  519.2 6.1 all_gather.146
  525.3 31.9 %all-gather.10 = bf16[2048,176]{0,1:T(8,128)(2,1)S(1)} all-gather(bf16[256,176]{0,1:T(8,128)(2,1)S(1)} %get-tuple-element.20), channel_id=12, replica_groups=mesh['grp'=8,'rep'=4] {'grp'}, dimensions={0}, use_global_device_ids=true | all-gather | bytes 811008 | tf_op jit(solution)/shard_map/all_gather | solution.py:16
  557.9 6.1 all_gather.151
  564.0 31.9 %all-gather.12 = bf16[2048,176]{0,1:T(8,128)(2,1)S(1)} all-gather(bf16[256,176]{0,1:T(8,128)(2,1)S(1)} %get-tuple-element.19), channel_id=14, replica_groups=mesh['grp'=8,'rep'=4] {'grp'}, dimensions={0}, use_global_device_ids=true | all-gather | bytes 811008 | tf_op jit(solution)/shard_map/all_gather | solution.py:16
  596.6 6.1 all_gather.156
  602.7 31.9 %all-gather.14 = bf16[2048,176]{0,1:T(8,128)(2,1)S(1)} all-gather(bf16[256,176]{0,1:T(8,128)(2,1)S(1)} %get-tuple-element.5), channel_id=16, replica_groups=mesh['grp'=8,'rep'=4] {'grp'}, dimensions={0}, use_global_device_ids=true | all-gather | bytes 811008 | tf_op jit(solution)/shard_map/all_gather | solution.py:16
  635.3 6.2 all_gather.161
  646.6 1.1 convolution_add_fusion.4
  (100 shorter events, 24.9 us)
Async XLA Ops:
  3.0 8.7 %copy-start.11 = (f32[32,24]{0,1:T(8,128)S(1)}, f32[32,24]{0,1:T(8,128)}, u32[]{:S(2)}) copy-start(f32[32,24]{0,1:T(8,128)} %param.7) | copy-start | bytes 9220
  3.0 326.1 %all-to-all-start = ((bf16[32,8,176]{2,0,1:T(8,128)(2,1)}), bf16[32,8,176]{2,0,1:T(8,128)(2,1)S(1)}, u32[]{:S(2)}, u32[]{:S(2)}) async-start(bf16[32,8,176]{2,0,1:T(8,128)(2,1)} %bitcast.126), calls=%async_computation | async-start | bytes 262144 | tf_op jit(solution)/shard_map/all_to_all | solution.py:111
  10.4 0.7 copy-start.12
  45.9 9.6 %copy-start.4 = (bf16[704,64]{0,1:T(8,128)(2,1)S(1)}, bf16[704,64]{0,1:T(8,128)(2,1)}, u32[]{:S(2)}) copy-start(bf16[704,64]{0,1:T(8,128)(2,1)} %param.11) | copy-start | bytes 270340
  49.2 0.7 copy-start.10
  325.5 1.5 copy-start
  326.3 1.5 copy-start.1
  327.0 1.2 copy-start.2
  327.8 1.2 copy-start.3
  635.3 6.2 copy-start.9
  641.5 0.9 copy-start.8
  642.4 0.9 copy-start.7
  643.3 0.9 copy-start.6
  644.2 0.9 copy-start.5
